TPU v7x, 256 devices: a whole 4x4x8 slice. The times are simulated.
256 devices in a mesh: expert: 32 (over y, x, core), tensor: 8 (over z).
Axes of the slice: x: 4, y: 4, z: 8, core: 2. Of those that a mesh axis runs over, the one named last changes fastest.
Arguments:
- tokens: bfloat16 [16384, 4096], P('expert', 'tensor'), may hold values from -36 to 36
- expert_ids: int32 [16384, 1], P('expert'), may hold values from 0 to 63; in each aligned block of 512 rows (0 to 511, 512 to 1023, ...) at most 16 rows name the same one
- gates: float32 [16384, 1], P('expert'), may hold values from 0.25 to 1
- expert_in: bfloat16 [64, 4096, 2048], P('expert', 'tensor'), may hold values from -0.09375 to 0.09375
- expert_out: bfloat16 [64, 2048, 4096], P('expert', None, 'tensor'), may hold values from -0.125 to 0.125
- norm_gain: float32 [4096], replicated, may hold values from 0.5 to 2
- up_weight: bfloat16 [4096, 8192], P('expert', 'tensor'), may hold values from -0.09375 to 0.09375
- down_weight: bfloat16 [4096, 8192], P('expert', 'tensor'), may hold values from -0.0625 to 0.0625
Outputs:
- layer_output: bfloat16 [16384, 4096], P('expert', 'tensor')
Inputs may be any that keep to these rules, and one draw needn't show every extreme that they name: `expert_ids`: among the 512 tokens of one block, at most 16 carry the same expert id; in some blocks one id is carried by exactly 16 tokens.
All inputs are finite; a program needn't handle non-finite values.
Results may differ from a plain program's by a relative error of at most 0.015.
Values may be sent and summed in bfloat16 or wider, within the bound.
No kernel may reach another device: no remote copies, remote signals or barrier semaphores. Data moves between devices by JAX's collectives and lax.ppermute only.
A program may use at most 128 MiB of HBM per device.

v0:
```python
import jax
import jax.numpy as jnp
from jax import lax
from jax.sharding import PartitionSpec as P

EXP_DEV = 2


def slot_table(expert_col, experts, capacity):
    expert = expert_col[:, 0]
    onehot = (expert[:, None] == jnp.arange(experts, dtype=jnp.int32)[None, :]).astype(jnp.int32)
    before = jnp.cumsum(onehot, axis=0) - onehot
    position = jnp.sum(before * onehot, axis=1)
    slot_index = expert * capacity + position
    selector = jnp.arange(experts * capacity, dtype=jnp.int32)[:, None] == slot_index[None, :]
    return selector.astype(jnp.bfloat16)


def trade(buffer):
    result = lax.all_to_all(buffer, "expert", split_axis=0, concat_axis=0, tiled=True)
    return result


def gather_rows(weight, combine, start_value):
    return combine(start_value, lax.all_gather(weight, "expert", axis=0, tiled=True), jnp.int32(0))


def shards(tokens, expert_ids, gates, expert_in, expert_out, norm_gain, up_weight, down_weight):
    token_count = tokens.shape[0]
    local_width = tokens.shape[1]
    groups = lax.axis_size("expert")
    experts = EXP_DEV * groups
    capacity = 2 * token_count // experts
    selector = slot_table(expert_ids, experts, capacity)
    outgoing = jnp.dot(selector, tokens, preferred_element_type=jnp.float32).astype(jnp.bfloat16)
    outgoing = outgoing.reshape(groups, EXP_DEV, capacity, local_width)
    arrived = trade(outgoing)
    partial_value = jnp.einsum(
        "sjcd,jdh->sjch", arrived, expert_in, preferred_element_type=jnp.float32
    )
    summed = lax.psum(partial_value.astype(jnp.bfloat16), "tensor").astype(jnp.float32)
    active = jax.nn.relu(summed).astype(jnp.bfloat16)
    produced = jnp.einsum(
        "sjch,jhd->sjcd", active, expert_out, preferred_element_type=jnp.float32
    ).astype(jnp.bfloat16)
    returned = trade(produced).reshape(experts * capacity, local_width)
    routed = lax.dot_general(
        selector, returned, (((0,), (0,)), ((), ())), preferred_element_type=jnp.float32
    )
    mixed = (tokens.astype(jnp.float32) + gates * routed).astype(jnp.bfloat16)
    whole = lax.all_gather(mixed, "tensor", axis=1, tiled=True)
    whole_f32 = whole.astype(jnp.float32)
    mean_square = jnp.mean(whole_f32 * whole_f32, axis=1, keepdims=True)
    normed = (whole_f32 * lax.rsqrt(mean_square + 1e-06) * norm_gain).astype(jnp.bfloat16)

    def add_up(carry, piece, start):
        return jnp.dot(normed, piece, preferred_element_type=jnp.float32)

    ffn_hidden = gather_rows(
        up_weight, add_up, jnp.zeros((token_count, up_weight.shape[1]), jnp.float32)
    )
    ffn_active = jax.nn.gelu(ffn_hidden, approximate=True).astype(jnp.bfloat16)

    def add_down(carry, piece, start):
        contribution = lax.dot_general(
            ffn_active, piece, (((1,), (1,)), ((), ())), preferred_element_type=jnp.float32
        )
        return contribution

    outputs = gather_rows(
        down_weight, add_down, jnp.zeros((token_count, whole.shape[1]), jnp.float32)
    )
    summed_out = lax.psum_scatter(
        outputs.astype(jnp.bfloat16), "tensor", scatter_dimension=1, tiled=True
    ).astype(jnp.float32)
    return (mixed.astype(jnp.float32) + summed_out).astype(jnp.bfloat16)


def solution(mesh):
    return jax.shard_map(
        shards,
        mesh=mesh,
        in_specs=(
            P("expert", "tensor"),
            P("expert", None),
            P("expert", None),
            P("expert", "tensor", None),
            P("expert", None, "tensor"),
            P(),
            P("expert", "tensor"),
            P("expert", "tensor"),
        ),
        out_specs=P("expert", "tensor"),
        check_vma=False,
    )
```

profile of v0, /device:TPU:1, one launch (start us, length us, event | category | flops | bytes accessed | tf_op | source)
XLA Modules:
  0.0 424.8 jit_solution(10991581283528540992)
XLA Ops:
  6.5 0.7 fusion.42
  7.2 1.2 reduce-window.6
  8.4 0.2 slice_reduce_fusion
  8.7 0.9 fusion.41
  9.7 0.9 multiply_add_fusion
  10.6 1.8 fusion.24
  12.4 25.6 %all_to_all.10 = bf16[32,2,16,512]{3,2,1,0:T(8,128)(2,1)S(1)} all-to-all(bf16[32,2,16,512]{3,2,1,0:T(8,128)(2,1)S(1)} %bitcast.50), channel_id=1, replica_groups=mesh['expert'=32,'tensor'=8] {'expert'}, dimensions={0} | all-to-all | bytes 2097152 | tf_op jit(solution)/shard_map/all_to_all | solution.py:20
  37.9 4.3 %convert_bitcast_fusion = bf16[32,2,16,2048]{3,2,0,1:T(8,128)(2,1)} fusion(bf16[2,512,2048]{2,1,0:T(8,128)(2,1)S(1)} %copy-done.1, bf16[32,2,16,512]{3,2,1,0:T(8,128)(2,1)S(1)} %all_to_all.10), kind=kOutput, calls=%fused_computation.15 | convolution fusion | flops 2149580800 | bytes 9437184 | tf_op jit(solution)/shard_map/sjcd,jdh->sjch/dot_general | solution.py:38
  42.2 0.0 all-reduce.2.cloned.1.call-update
  42.3 0.0 all-gather.4.cloned.1.call-start
  42.3 108.1 %all-reduce.2.cloned.1.call-done = bf16[32,2,16,2048]{3,2,0,1:T(8,128)(2,1)} async-done(((bf16[32,2,16,2048]{3,2,0,1:T(8,128)(2,1)}), bf16[32,2,16,2048]{3,2,0,1:T(8,128)(2,1)}) %all-reduce.2.cloned.1.call-update) | async-done | bytes 4194320 | tf_op jit(solution)/shard_map/psum | solution.py:41
  150.4 5.8 %fusion.30 = bf16[32,2,16,512]{3,2,0,1:T(8,128)(2,1)S(1)} fusion(bf16[2,2048,512]{2,1,0:T(8,128)(2,1)} %param.12, bf16[32,2,16,2048]{3,2,0,1:T(8,128)(2,1)} %all-reduce.2.cloned.1.call-done), kind=kOutput, calls=%fused_computation.30 | convolution fusion | flops 2154299392 | bytes 9437184 | tf_op jit(solution)/shard_map/sjch,jhd->sjcd/dot_general | solution.py:43
  156.2 0.0 copy-start.2
  156.2 0.0 copy-start.4
  156.2 0.1 copy.16
  156.3 24.6 %all_to_all.11 = bf16[32,2,16,512]{3,2,1,0:T(8,128)(2,1)S(1)} all-to-all(bf16[32,2,16,512]{3,2,1,0:T(8,128)(2,1)S(1)} %copy.16), channel_id=1, replica_groups=mesh['expert'=32,'tensor'=8] {'expert'}, dimensions={0} | all-to-all | bytes 2097152 | tf_op jit(solution)/shard_map/all_to_all | solution.py:20
  180.9 1.6 fusion.35
  182.5 0.0 all-gather.4.cloned.1.call-update
  182.5 0.0 all-gather.6.cloned.1.call-start
  182.6 0.7 all-gather.6.cloned.1.call-update
  183.3 0.0 all-gather.8.cloned.1.call-start
  183.3 0.5 all-gather.8.cloned.1.call-update
  183.8 0.2 reduce-scatter.2.cloned.1.call-start
  184.1 48.4 %all-gather.4.cloned.1.call-done = bf16[512,4096]{1,0:T(8,128)(2,1)} async-done(((bf16[512,512]{1,0:T(8,128)(2,1)}), bf16[512,4096]{1,0:T(8,128)(2,1)}) %all-gather.4.cloned.1.call-update) | async-done | bytes 4194320 | tf_op jit(solution)/shard_map/all_gather | solution.py:51
  232.4 3.1 fusion
  235.5 56.4 %all-gather.6.cloned.1.call-done = bf16[4096,1024]{1,0:T(8,128)(2,1)} async-done(((bf16[128,1024]{1,0:T(8,128)(2,1)}), bf16[4096,1024]{1,0:T(8,128)(2,1)}) %all-gather.6.cloned.1.call-update) | async-done | bytes 8388624 | tf_op jit(solution)/shard_map/all_gather | solution.py:25
  292.0 9.6 %fusion.21 = bf16[512,1024]{1,0:T(8,128)(2,1)S(1)} fusion(bf16[4096,1024]{1,0:T(8,128)(2,1)} %all-gather.6.cloned.1.call-done, bf16[512,4096]{1,0:T(8,128)(2,1)} %all-gather.4.cloned.1.call-done, f32[4096]{0:T(1024)S(1)} %copy-done.3, f32[512]{0:T(512)S(1)} %add_rsqrt_fusion), kind=kOutput, calls=%fused_computation.24 | convolution fusion | flops 4308074496 | bytes 13649920 | tf_op jit(solution)/shard_map/dot_general | solution.py:57
  301.6 50.4 %all-gather.8.cloned.1.call-done = bf16[4096,1024]{1,0:T(8,128)(2,1)} async-done(((bf16[128,1024]{1,0:T(8,128)(2,1)}), bf16[4096,1024]{1,0:T(8,128)(2,1)}) %all-gather.8.cloned.1.call-update) | async-done | bytes 8388624 | tf_op jit(solution)/shard_map/all_gather | solution.py:25
  352.0 9.5 %convolution_convert_fusion = bf16[512,4096]{1,0:T(8,128)(2,1)} fusion(bf16[512,1024]{1,0:T(8,128)(2,1)S(1)} %fusion.21, bf16[4096,1024]{1,0:T(8,128)(2,1)} %all-gather.8.cloned.1.call-done), kind=kOutput, calls=%fused_computation.6 | convolution fusion | flops 4297064448 | bytes 13631488 | tf_op jit(solution)/shard_map/dot_general | solution.py:65
  361.5 0.0 reduce-scatter.2.cloned.1.call-update
  361.5 54.7 %reduce-scatter.2.cloned.1.call-done = bf16[512,512]{1,0:T(8,128)(2,1)} async-done(((bf16[512,4096]{1,0:T(8,128)(2,1)}), bf16[512,512]{1,0:T(8,128)(2,1)}) %reduce-scatter.2.cloned.1.call-update) | async-done | bytes 524304 | tf_op jit(solution)/shard_map/reduce_scatter | solution.py:73
  416.3 2.0 add_convert_fusion
  (12 shorter events, 0.1 us)
Async XLA Ops:
  6.5 143.8 %all-reduce.2.cloned.1.call-start = ((), (), s32[]{:S(2)}) async-start(), calls=%async_computation.3 | async-start | bytes 8388608 | tf_op jit(solution)/shard_map/psum | solution.py:41
  8.7 29.2 %copy-start.1 = (bf16[2,512,2048]{2,1,0:T(8,128)(2,1)S(1)}, bf16[2,512,2048]{2,1,0:T(8,128)(2,1)}, u32[]{:S(2)}) copy-start(bf16[2,512,2048]{2,1,0:T(8,128)(2,1)} %param.11) | copy-start | bytes 12582916
  42.3 190.2 %all-gather.4.cloned.1.call-start = ((), (), s32[]{:S(2)}) async-start(), calls=%async_computation.4 | async-start | bytes 4718592 | tf_op jit(solution)/shard_map/all_gather | solution.py:51
  156.2 24.7 %copy-start.2 = (bf16[512,512]{1,0:T(8,128)(2,1)S(1)}, bf16[512,512]{1,0:T(8,128)(2,1)}, u32[]{:S(2)}) copy-start(bf16[512,512]{1,0:T(8,128)(2,1)} %param.8) | copy-start | bytes 1572868
  156.2 24.7 %copy-start.4 = (f32[512,1]{0,1:T(1,128)S(1)}, f32[512,1]{0,1:T(1,128)}, u32[]{:S(2)}) copy-start(f32[512,1]{0,1:T(1,128)} %param.10) | copy-start | bytes 6148
  180.9 111.0 %copy-start.3 = (f32[4096]{0:T(1024)S(1)}, f32[4096]{0:T(1024)}, u32[]{:S(2)}) copy-start(f32[4096]{0:T(1024)} %param.13) | copy-start | bytes 49156
  182.5 109.4 %all-gather.6.cloned.1.call-start = ((), (), s32[]{:S(2)}) async-start(), calls=%async_computation.5 | async-start | bytes 8650752 | tf_op jit(solution)/shard_map/all_gather | solution.py:25
  183.3 168.7 %all-gather.8.cloned.1.call-start = ((), (), s32[]{:S(2)}) async-start(), calls=%async_computation.6 | async-start | bytes 8650752 | tf_op jit(solution)/shard_map/all_gather | solution.py:25
  183.8 232.4 %reduce-scatter.2.cloned.1.call-start = ((), (), s32[]{:S(2)}) async-start(), calls=%async_computation.7 | async-start | bytes 4718592 | tf_op jit(solution)/shard_map/reduce_scatter | solution.py:73
  361.5 54.8 %copy-start = (bf16[512,512]{1,0:T(8,128)(2,1)S(1)}, bf16[512,512]{1,0:T(8,128)(2,1)}, u32[]{:S(2)}) copy-start(bf16[512,512]{1,0:T(8,128)(2,1)} %fusion.35) | copy-start | bytes 1572868
Sparse Core Ops, SparseCore 0:
  42.4 107.9 all-reduce.1
  182.6 49.7 all-gather.3
  235.0 56.9 all-gather.5
  294.4 57.5 all-gather.7
  361.6 54.5 reduce-scatter.1
where the time goes:
time: 425 us
  waiting for transfers between devices  319 us (75%)
  blocking collectives  50.2 us (12%)
  matrix products  32.6 us (8%)
  between operations  13.2 us (3%)
  other arithmetic  8.86 us (2%)
    psum x1, waiting for transfers between devices, shards(): lax.psum(partial_value.astype(jnp.bfloat16), 'tensor').astype(jnp.float32)  108 us
    all_gather x2, waiting for transfers between devices, gather_rows(): lax.all_gather(weight, 'expert', axis=0, tiled=True)  107 us
    reduce_scatter x1, waiting for transfers between devices, shards(): lax.psum_scatter(outputs.astype(jnp.bfloat16), 'tensor', scatter_dimensio...  54.7 us
    all_to_all x2, blocking collectives, trade(): lax.all_to_all(buffer, 'expert', split_axis=0, concat_axis=0, tiled=True)  50.2 us
    all_gather x1, waiting for transfers between devices, shards(): whole = lax.all_gather(mixed, 'tensor', axis=1, tiled=True)  48.4 us
    dot_general x1, matrix products, add_up(): return jnp.dot(normed, piece, preferred_element_type=jnp.float32)  9.58 us
    dot_general x1, matrix products, add_down(): lax.dot_general(ffn_active, piece, (((1,), (1,)), ((), ())), preferred_el...  9.54 us
  transfers between devices with their start and end apart: 5, of which 5 were waited for; matrix products, arithmetic and copies ran while one was open for 3% of the time, Pallas kernels for 0%

commit v1 on v0

--- a/solution.py
+++ b/solution.py
@@ -38,7 +38,9 @@
     partial_value = jnp.einsum(
         "sjcd,jdh->sjch", arrived, expert_in, preferred_element_type=jnp.float32
     )
-    summed = lax.psum(partial_value.astype(jnp.bfloat16), "tensor").astype(jnp.float32)
+    summed = jnp.sum(lax.all_gather(partial_value.astype(jnp.bfloat16), "tensor"), axis=0).astype(
+        jnp.float32
+    )
     active = jax.nn.relu(summed).astype(jnp.bfloat16)
     produced = jnp.einsum(
         "sjch,jhd->sjcd", active, expert_out, preferred_element_type=jnp.float32

time: 425 us -> 660 us (1.55)
  waiting for transfers between devices: 319 us -> 540 us
  other arithmetic: 8.86 us -> 23.1 us
    all_gather x0 -> x1, waiting for transfers between devices: none -> 329 us  [shards(): lax.all_gather(partial_value.astype(jnp.bfloat16), 'tensor')]
    psum x1 -> x0, waiting for transfers between devices: 108 us -> none  [shards(): lax.psum(partial_value.astype(jnp.bfloat16), 'tensor').astype(jnp.float32)]
    reduce_sum x0 -> x1, other arithmetic: none -> 14.2 us  [shards(): jnp.sum(lax.all_gather(partial_value.astype(jnp.bfloat16), 'tensor'), axi...]
  transfers between devices with their start and end apart: 5 -> 5, of which waited for: 5 -> 5; matrix products, arithmetic and copies ran while one was open for 3% -> 2% of each run, Pallas kernels for 0% -> 0%
where the time goes in v1:
time: 660 us
  waiting for transfers between devices  540 us (82%)
  blocking collectives  50.2 us (8%)
  matrix products  32.7 us (5%)
  other arithmetic  23.1 us (4%)
  between operations  13.2 us (2%)
    all_gather x1, waiting for transfers between devices, shards(): lax.all_gather(partial_value.astype(jnp.bfloat16), 'tensor')  329 us
    all_gather x2, waiting for transfers between devices, gather_rows(): lax.all_gather(weight, 'expert', axis=0, tiled=True)  107 us
    reduce_scatter x1, waiting for transfers between devices, shards(): lax.psum_scatter(outputs.astype(jnp.bfloat16), 'tensor', scatter_dimensio...  54.7 us
    all_to_all x2, blocking collectives, trade(): lax.all_to_all(buffer, 'expert', split_axis=0, concat_axis=0, tiled=True)  50.2 us
    all_gather x1, waiting for transfers between devices, shards(): whole = lax.all_gather(mixed, 'tensor', axis=1, tiled=True)  48.3 us
    reduce_sum x1, other arithmetic, shards(): jnp.sum(lax.all_gather(partial_value.astype(jnp.bfloat16), 'tensor'), axi...  14.2 us
  transfers between devices with their start and end apart: 5, of which 5 were waited for; matrix products, arithmetic and copies ran while one was open for 2% of the time, Pallas kernels for 0%

profile of v1, /device:TPU:1, one launch (start us, length us, event | category | flops | bytes accessed | tf_op | source)
XLA Modules:
  0.0 660.1 jit_solution(4898327029020504856)
XLA Ops:
  6.5 0.7 fusion.42
  7.2 1.2 reduce-window.6
  8.4 0.2 slice_reduce_fusion
  8.7 0.9 fusion.41
  9.7 0.9 multiply_add_fusion
  10.6 1.8 fusion.24
  12.4 25.6 %all_to_all.10 = bf16[32,2,16,512]{3,2,1,0:T(8,128)(2,1)S(1)} all-to-all(bf16[32,2,16,512]{3,2,1,0:T(8,128)(2,1)S(1)} %bitcast.52), channel_id=1, replica_groups=mesh['expert'=32,'tensor'=8] {'expert'}, dimensions={0} | all-to-all | bytes 2097152 | tf_op jit(solution)/shard_map/all_to_all | solution.py:20
  37.9 4.4 convert_bitcast_fusion
  42.3 0.0 all-gather.12.cloned.1.call-update
  42.3 0.0 all-gather.6.cloned.1.call-start
  42.4 329.1 %all-gather.12.cloned.1.call-done = bf16[256,2,16,2048]{3,2,0,1:T(8,128)(2,1)} async-done(((bf16[32,2,16,2048]{3,2,0,1:T(8,128)(2,1)}), bf16[256,2,16,2048]{3,2,0,1:T(8,128)(2,1)}) %all-gather.12.cloned.1.call-update) | async-done | bytes 33554448 | tf_op jit(solution)/shard_map/all_gather | solution.py:41
  371.5 14.2 %reduce_sum.31 = bf16[32,2,16,2048]{3,2,0,1:T(8,128)(2,1)} reduce(bf16[8,32,2,16,2048]{4,3,1,0,2:T(8,128)(2,1)} %bitcast.50, bf16[]{:T(256)} %constant.7.clone.1), dimensions={0}, to_apply=%region_3.4 | reduce | flops 14680064 | bytes 37748736 | tf_op jit(solution)/shard_map/reduce_sum | solution.py:41
  385.8 5.8 fusion.30
  391.6 0.0 copy-start.2
  391.6 0.1 copy.15
  391.7 24.6 %all_to_all.11 = bf16[32,2,16,512]{3,2,1,0:T(8,128)(2,1)S(1)} all-to-all(bf16[32,2,16,512]{3,2,1,0:T(8,128)(2,1)S(1)} %copy.15), channel_id=1, replica_groups=mesh['expert'=32,'tensor'=8] {'expert'}, dimensions={0} | all-to-all | bytes 2097152 | tf_op jit(solution)/shard_map/all_to_all | solution.py:20
  416.3 1.6 fusion.35
  417.9 0.0 all-gather.6.cloned.1.call-update
  417.9 0.0 all-gather.8.cloned.1.call-start
  417.9 0.7 all-gather.8.cloned.1.call-update
  418.6 0.0 all-gather.10.cloned.1.call-start
  418.7 0.5 all-gather.10.cloned.1.call-update
  419.2 0.2 reduce-scatter.2.cloned.1.call-start
  419.4 48.3 %all-gather.6.cloned.1.call-done = bf16[512,4096]{1,0:T(8,128)(2,1)} async-done(((bf16[512,512]{1,0:T(8,128)(2,1)}), bf16[512,4096]{1,0:T(8,128)(2,1)}) %all-gather.6.cloned.1.call-update) | async-done | bytes 4194320 | tf_op jit(solution)/shard_map/all_gather | solution.py:53
  467.7 3.1 fusion
  470.8 56.4 %all-gather.8.cloned.1.call-done = bf16[4096,1024]{1,0:T(8,128)(2,1)} async-done(((bf16[128,1024]{1,0:T(8,128)(2,1)}), bf16[4096,1024]{1,0:T(8,128)(2,1)}) %all-gather.8.cloned.1.call-update) | async-done | bytes 8388624 | tf_op jit(solution)/shard_map/all_gather | solution.py:25
  527.3 9.6 %fusion.21 = bf16[512,1024]{1,0:T(8,128)(2,1)S(1)} fusion(bf16[4096,1024]{1,0:T(8,128)(2,1)} %all-gather.8.cloned.1.call-done, bf16[512,4096]{1,0:T(8,128)(2,1)} %all-gather.6.cloned.1.call-done, f32[4096]{0:T(1024)S(1)} %copy-done.3, f32[512]{0:T(512)S(1)} %add_rsqrt_fusion), kind=kOutput, calls=%fused_computation.24 | convolution fusion | flops 4308074496 | bytes 13649920 | tf_op jit(solution)/shard_map/dot_general | solution.py:59
  536.9 50.4 %all-gather.10.cloned.1.call-done = bf16[4096,1024]{1,0:T(8,128)(2,1)} async-done(((bf16[128,1024]{1,0:T(8,128)(2,1)}), bf16[4096,1024]{1,0:T(8,128)(2,1)}) %all-gather.10.cloned.1.call-update) | async-done | bytes 8388624 | tf_op jit(solution)/shard_map/all_gather | solution.py:25
  587.3 9.5 %convolution_convert_fusion = bf16[512,4096]{1,0:T(8,128)(2,1)} fusion(bf16[512,1024]{1,0:T(8,128)(2,1)S(1)} %fusion.21, bf16[4096,1024]{1,0:T(8,128)(2,1)} %all-gather.10.cloned.1.call-done), kind=kOutput, calls=%fused_computation.6 | convolution fusion | flops 4297064448 | bytes 13631488 | tf_op jit(solution)/shard_map/dot_general | solution.py:67
  596.8 0.0 reduce-scatter.2.cloned.1.call-update
  596.9 54.7 %reduce-scatter.2.cloned.1.call-done = bf16[512,512]{1,0:T(8,128)(2,1)} async-done(((bf16[512,4096]{1,0:T(8,128)(2,1)}), bf16[512,512]{1,0:T(8,128)(2,1)}) %reduce-scatter.2.cloned.1.call-update) | async-done | bytes 524304 | tf_op jit(solution)/shard_map/reduce_scatter | solution.py:75
  651.6 2.0 add_convert_fusion
  (13 shorter events, 0.1 us)
Async XLA Ops:
  6.5 365.0 %all-gather.12.cloned.1.call-start = ((), (), s32[]{:S(2)}) async-start(), calls=%async_computation.7 | async-start | bytes 37748736 | tf_op jit(solution)/shard_map/all_gather | solution.py:41
  8.7 29.2 %copy-start.1 = (bf16[2,512,2048]{2,1,0:T(8,128)(2,1)S(1)}, bf16[2,512,2048]{2,1,0:T(8,128)(2,1)}, u32[]{:S(2)}) copy-start(bf16[2,512,2048]{2,1,0:T(8,128)(2,1)} %param.11) | copy-start | bytes 12582916
  42.3 425.4 %all-gather.6.cloned.1.call-start = ((), (), s32[]{:S(2)}) async-start(), calls=%async_computation.3 | async-start | bytes 4718592 | tf_op jit(solution)/shard_map/all_gather | solution.py:53
  391.6 24.7 %copy-start.2 = (bf16[512,512]{1,0:T(8,128)(2,1)S(1)}, bf16[512,512]{1,0:T(8,128)(2,1)}, u32[]{:S(2)}) copy-start(bf16[512,512]{1,0:T(8,128)(2,1)} %param.8) | copy-start | bytes 1572868
  391.6 24.7 %copy-start.4 = (f32[512,1]{0,1:T(1,128)S(1)}, f32[512,1]{0,1:T(1,128)}, u32[]{:S(2)}) copy-start(f32[512,1]{0,1:T(1,128)} %param.10) | copy-start | bytes 6148
  416.3 111.0 %copy-start.3 = (f32[4096]{0:T(1024)S(1)}, f32[4096]{0:T(1024)}, u32[]{:S(2)}) copy-start(f32[4096]{0:T(1024)} %param.13) | copy-start | bytes 49156
  417.9 109.4 %all-gather.8.cloned.1.call-start = ((), (), s32[]{:S(2)}) async-start(), calls=%async_computation.4 | async-start | bytes 8650752 | tf_op jit(solution)/shard_map/all_gather | solution.py:25
  418.6 168.7 %all-gather.10.cloned.1.call-start = ((), (), s32[]{:S(2)}) async-start(), calls=%async_computation.5 | async-start | bytes 8650752 | tf_op jit(solution)/shard_map/all_gather | solution.py:25
  419.2 232.4 %reduce-scatter.2.cloned.1.call-start = ((), (), s32[]{:S(2)}) async-start(), calls=%async_computation.6 | async-start | bytes 4718592 | tf_op jit(solution)/shard_map/reduce_scatter | solution.py:75
  596.8 54.8 %copy-start = (bf16[512,512]{1,0:T(8,128)(2,1)S(1)}, bf16[512,512]{1,0:T(8,128)(2,1)}, u32[]{:S(2)}) copy-start(bf16[512,512]{1,0:T(8,128)(2,1)} %fusion.35) | copy-start | bytes 1572868
Sparse Core Ops, SparseCore 0:
  42.5 329.0 all-gather.11
  418.0 49.6 all-gather.5
  470.3 56.9 all-gather.7
  529.7 57.5 all-gather.9
  597.0 54.5 reduce-scatter.1
